TPU v7x, 256 devices: a whole 4x4x8 slice. The times are simulated.
256 devices in a mesh: ctx: 64 (over x, z, core), lat: 4 (over y).
Axes of the slice: x: 4, y: 4, z: 8, core: 2. Of those that a mesh axis runs over, the one named last changes fastest.
Arguments:
- token_ids: int32 [32768], P('ctx'), may hold values from 0 to 255
- latent_offset: int32 [1], replicated, may hold values from 31616 to 31744
- embed_table: bfloat16 [256, 2048], replicated, may hold values from -6 to 6
- cross_q: bfloat16 [2048, 2048], P('ctx', 'lat')
- cross_kv: bfloat16 [2, 2048, 2048], P(None, 'ctx', 'lat')
- cross_out: bfloat16 [2048, 2048], P('lat'), may hold values from -0.375 to 0.375
- self_qkv: bfloat16 [3, 2048, 2048], P(None, None, 'lat')
- self_out: bfloat16 [2048, 2048], P('lat'), may hold values from -0.25 to 0.25
- mlp_in: bfloat16 [2048, 8192], P(None, 'ctx'), may hold values from -0.125 to 0.125
- mlp_out: bfloat16 [8192, 2048], P('ctx'), may hold values from -0.0625 to 0.0625
Outputs:
- latent_out: bfloat16 [4, 256, 2048], P('lat', 'ctx')
Inputs may be any that keep to these rules, and one draw needn't show every extreme that they name: `latent_offset`: the latent rows lie inside the context.
All inputs are finite; a program needn't handle non-finite values.
Results may differ from a plain program's by a relative error of at most 0.014.
Values may be sent and summed in bfloat16 or wider, within the bound.
A program may use at most 128 MiB of HBM per device.

v0:
```python
import math
import jax
import jax.numpy as jnp
from jax import lax
from jax.sharding import PartitionSpec as P

HD = 128
LATENTS = 1024
EPSILON = 1e-06
MASKED = -1e30


def sent_to_all(array, axis):
    count = lax.axis_size(axis)
    return lax.all_to_all(
        jnp.broadcast_to(array[None], (count, *array.shape)), axis, 0, 0, tiled=True
    )


def laid_out(pieces, dim):
    pieces = jnp.moveaxis(pieces, 0, dim)
    shape = pieces.shape
    return pieces.reshape(*shape[:dim], shape[dim] * shape[dim + 1], *shape[dim + 2 :])


def gathered_copies(array, axis, dim):
    pieces = sent_to_all(array, axis)
    return laid_out(pieces, dim)


def side_by_side(arrays, axis, split_dim, concat_dim, along):
    ends, at = ([], 0)
    for a in arrays[:-1]:
        at += a.shape[along]
        ends.append(at)
    both = jnp.concatenate(arrays, axis=along)
    return tuple(
        jnp.split(
            lax.all_to_all(both, axis, split_axis=split_dim, concat_axis=concat_dim, tiled=True),
            ends,
            axis=along,
        )
    )


def of_everyone(array, axis):
    return sent_to_all(array, axis).sum(axis=0)


def side_by_side_2(arrays, axis, dim, along):
    ends, at = ([], 0)
    for a in arrays[:-1]:
        at += a.shape[along]
        ends.append(at)
    both = jnp.concatenate(arrays, axis=along)
    return tuple(jnp.split(lax.all_gather(both, axis, axis=dim, tiled=True), ends, axis=along))


def over_copies(array, axis):
    everything = sent_to_all(array, axis)
    return jnp.sum(everything.astype(jnp.float32), axis=0)


def in_blocks(array, dim, count):
    before, after = (array.shape[:dim], array.shape[dim + 1 :])
    return jnp.moveaxis(array.reshape(*before, count, -1, *after), dim, 0)


def sent_and_summed(array, axis, dim):
    count = lax.axis_size(axis)
    pieces = lax.all_to_all(in_blocks(array, dim, count), axis, 0, 0, tiled=True)
    return jnp.sum(pieces, axis=0)


def rms_normalize(values):
    return values * lax.rsqrt(jnp.mean(values * values, axis=-1, keepdims=True) + EPSILON)


def sinusoid(places, width):
    index = jnp.arange(width // 2).astype(jnp.float32)
    rates = jnp.exp(index * (-2.0 * math.log(10000.0) / width))
    angles = places.astype(jnp.float32)[:, None] * rates[None, :]
    return jnp.stack([jnp.sin(angles), jnp.cos(angles)], axis=-1).reshape(places.shape[0], width)


def embed_rows(token_rows, table, places):
    vocab_range = jnp.arange(table.shape[0], dtype=jnp.int32)
    one_hot = (token_rows[:, None] == vocab_range[None, :]).astype(jnp.bfloat16)
    looked = jnp.dot(one_hot, table, preferred_element_type=jnp.float32)
    return rms_normalize(looked + sinusoid(places, table.shape[1])).astype(jnp.bfloat16)


def block_attention(queries, keys, values, blocked, head_size):
    scale = 1.0 / math.sqrt(head_size)
    head_count = queries.shape[1] // head_size
    query_rows = queries.shape[0]
    key_rows = keys.shape[0]
    query_heads = jnp.transpose(queries.reshape(query_rows, head_count, head_size), (1, 0, 2))
    key_heads = jnp.transpose(keys.reshape(key_rows, head_count, head_size), (1, 0, 2))
    value_heads = jnp.transpose(values.reshape(key_rows, head_count, head_size), (1, 0, 2))

    def one_head(operands):
        query, key, value = operands
        scores = (
            lax.dot_general(
                query, key, (((1,), (1,)), ((), ())), preferred_element_type=jnp.float32
            )
            * scale
        )
        scores = jnp.where(blocked, MASKED, scores)
        peak = jnp.max(scores, axis=1)
        weights = jnp.exp(scores - peak[:, None]).astype(jnp.bfloat16)
        total = jnp.sum(weights.astype(jnp.float32), axis=1)
        output = jnp.dot(weights, value, preferred_element_type=jnp.float32)
        return (peak, total, output)

    maxima, totals, outputs = lax.map(one_head, (query_heads, key_heads, value_heads))
    merged = jnp.transpose(outputs, (1, 0, 2)).reshape(query_rows, head_count * head_size)
    return (jnp.transpose(maxima), jnp.transpose(totals), merged)


def per_device(
    token_ids,
    latent_offset,
    embed_table,
    cross_q,
    cross_kv,
    cross_out,
    self_qkv,
    self_out,
    mlp_in,
    mlp_out,
):
    context_count = lax.axis_size("ctx")
    group_count = lax.axis_size("lat")
    context_index = lax.axis_index("ctx")
    group_index = lax.axis_index("lat")
    block_length = token_ids.shape[0]
    head_size = HD
    local_width = cross_q.shape[1]
    local_heads = local_width // head_size
    width = embed_table.shape[1]
    offset = latent_offset[0]
    latent_count = LATENTS
    row_count = latent_count // context_count
    group_rows = latent_count // group_count
    places = context_index * block_length + jnp.arange(block_length, dtype=jnp.int32)
    context = embed_rows(token_ids, embed_table, places)
    piece = lax.all_gather(cross_kv, "ctx", axis=1, tiled=True)
    columns = context
    key_sum = jnp.dot(columns, piece[0], preferred_element_type=jnp.float32)
    value_sum = jnp.dot(columns, piece[1], preferred_element_type=jnp.float32)
    keys = key_sum.astype(jnp.bfloat16)
    values = value_sum.astype(jnp.bfloat16)
    every_token = gathered_copies(token_ids, "ctx", 0)
    latent_tokens = lax.dynamic_slice_in_dim(every_token, offset, latent_count, 0)
    latent_places = offset + jnp.arange(latent_count, dtype=jnp.int32)
    latent = embed_rows(latent_tokens, embed_table, latent_places)
    columns = latent
    query_sum = jnp.dot(
        columns, gathered_copies(cross_q, "ctx", 0), preferred_element_type=jnp.float32
    )
    queries = query_sum.astype(jnp.bfloat16)
    blocked = places[None, :] > latent_places[:, None]
    maxima, totals, outputs = block_attention(queries, keys, values, blocked, head_size)
    row_start = context_index * row_count
    came_max, came_total, came_out = side_by_side(
        (maxima[:, None, :], totals[:, None, :], outputs[:, None, :]), "ctx", 0, 1, 2
    )
    peak = jnp.max(came_max, axis=1, keepdims=True)
    factor = jnp.exp(came_max - peak)
    own_totals = jnp.sum(came_total * factor, axis=1)
    spread = (
        came_out.reshape(row_count, context_count, local_heads, head_size) * factor[:, :, :, None]
    )
    own_outputs = jnp.sum(spread, axis=1).reshape(row_count, local_width)
    attended = (own_outputs / jnp.repeat(own_totals, head_size, axis=1)).astype(jnp.bfloat16)
    own_latent = lax.dynamic_slice_in_dim(latent, row_start, row_count, 0).astype(jnp.float32)
    first_stream = own_latent + of_everyone(
        jnp.dot(attended, cross_out, preferred_element_type=jnp.float32), "lat"
    )
    self_normed = rms_normalize(first_stream).astype(jnp.bfloat16)
    self_queries = jnp.dot(self_normed, self_qkv[0], preferred_element_type=jnp.float32).astype(
        jnp.bfloat16
    )
    self_keys = jnp.dot(self_normed, self_qkv[1], preferred_element_type=jnp.float32).astype(
        jnp.bfloat16
    )
    self_values = jnp.dot(self_normed, self_qkv[2], preferred_element_type=jnp.float32).astype(
        jnp.bfloat16
    )
    all_keys, all_values = side_by_side_2((self_keys, self_values), "ctx", 0, 1)
    own_places = row_start + jnp.arange(row_count, dtype=jnp.int32)
    later = jnp.arange(latent_count, dtype=jnp.int32)[None, :] > own_places[:, None]
    self_peak, self_totals, self_outputs = block_attention(
        self_queries, all_keys, all_values, later, head_size
    )
    self_attended = (self_outputs / jnp.repeat(self_totals, head_size, axis=1)).astype(jnp.bfloat16)
    second_stream = first_stream + over_copies(
        jnp.dot(self_attended, self_out, preferred_element_type=jnp.float32).astype(jnp.bfloat16),
        "lat",
    ).astype(jnp.float32)
    mlp_normed = rms_normalize(second_stream).astype(jnp.bfloat16)
    gathered = lax.all_gather(mlp_normed, "ctx", axis=0, tiled=True)
    group_input = lax.dynamic_slice_in_dim(gathered, group_index * group_rows, group_rows, 0)
    pre_hidden = jnp.dot(group_input, mlp_in, preferred_element_type=jnp.float32)
    hidden = jax.nn.gelu(pre_hidden, approximate=True).astype(jnp.bfloat16)
    place = context_index * row_count - group_index * group_rows
    inside = jnp.logical_and(place >= 0, place < group_rows)
    residual = jnp.zeros((group_rows, width), jnp.float32)
    residual = lax.dynamic_update_slice_in_dim(
        residual, second_stream, jnp.clip(place, 0, group_rows - row_count), 0
    )
    residual = jnp.where(inside, residual, 0.0)
    result = sent_and_summed(
        jnp.dot(hidden, mlp_out, preferred_element_type=jnp.float32) + residual, "ctx", 0
    )
    return result.astype(jnp.bfloat16)[None]


def solution(mesh):
    placed = (
        P("ctx"),
        P(),
        P(),
        P("ctx", "lat"),
        P(None, "ctx", "lat"),
        P("lat", None),
        P(None, None, "lat"),
        P("lat", None),
        P(None, "ctx"),
        P("ctx", None),
    )
    return jax.shard_map(
        per_device, mesh=mesh, in_specs=placed, out_specs=P("lat", "ctx", None), check_vma=False
    )
```

profile of v0, /device:TPU:1, one launch (start us, length us, event | category | flops | bytes accessed | tf_op | source)
XLA Modules:
  0.0 527.8 jit_solution(14020587515841500525)
XLA Ops:
  8.0 23.1 %all_to_all.44 = s32[64,1,512]{2,1,0:T(1,128)S(1)} all-to-all(s32[64,1,512]{2,1,0:T(1,128)S(1)} %broadcast_in_dim.52), channel_id=1, replica_groups=mesh['ctx'=64,'lat'=4] {'ctx'}, dimensions={0} | all-to-all | bytes 262144 | tf_op jit(solution)/shard_map/all_to_all | solution.py:15
  33.6 5.8 %all-to-all-start.1 = ((bf16[64,32,512]{2,1,0:T(8,128)(2,1)}), bf16[64,32,512]{2,1,0:T(8,128)(2,1)}, u32[]{:S(2)}, u32[]{:S(2)}) async-start(bf16[64,32,512]{2,1,0:T(8,128)(2,1)} %broadcast_in_dim.54), calls=%async_computation.1 | async-start | bytes 4194304 | tf_op jit(solution)/shard_map/all_to_all | solution.py:15
  40.1 14.9 %multiply_sine_fusion = (f32[1024,1024,1]{1,0,2:T(8,128)S(1)}, f32[1024,1024,1]{1,0,2:T(8,128)S(1)}) fusion(f32[1024]{0:T(1024)S(1)} %multiply_exponential_fusion, f32[1024]{0:T(1024)S(1)} %get-tuple-element.184), kind=kLoop, calls=%fused_computation.36 | loop fusion | flops 1048576 | bytes 8396800 | tf_op jit(solution)/shard_map/sin | solution.py:83
  55.0 4.1 pad_maximum_fusion
  59.0 13.6 %copy.62 = f32[1024,1024,2]{0,2,1:T(2,128)} copy(f32[1024,1024,2]{1,0,2:T(8,128)} %pad_maximum_fusion) | data formatting | bytes 16777216 | tf_op jit(solution)/shard_map/stack | solution.py:83
  72.6 10.9 %reshape.308 = f32[1024,2048]{0,1:T(8,128)} reshape(f32[1024,1024,2]{0,2,1:T(2,128)} %copy.62) | data formatting | bytes 16777216 | tf_op jit(solution)/shard_map/reshape | solution.py:83
  83.5 9.7 %copy.63 = f32[1024,2048]{1,0:T(8,128)} copy(f32[1024,2048]{0,1:T(8,128)} %reshape.308) | data formatting | bytes 16777216 | tf_op jit(solution)/shard_map/reshape | solution.py:83
  93.2 7.3 %multiply_sine_fusion.1 = (f32[512,1024,1]{1,0,2:T(8,128)S(1)}, f32[512,1024,1]{1,0,2:T(8,128)S(1)}) fusion(f32[1024]{0:T(1024)S(1)} %multiply_exponential_fusion, f32[512]{0:T(512)S(1)} %get-tuple-element.186), kind=kLoop, calls=%fused_computation.43 | loop fusion | flops 524288 | bytes 4200448 | tf_op jit(solution)/shard_map/sin | solution.py:83
  102.8 7.3 %copy.65 = f32[512,1024,2]{0,2,1:T(2,128)} copy(f32[512,1024,2]{1,0,2:T(8,128)} %pad_maximum_fusion.1) | data formatting | bytes 8388608 | tf_op jit(solution)/shard_map/stack | solution.py:83
  110.1 6.1 %reshape.311 = f32[512,2048]{0,1:T(8,128)} reshape(f32[512,1024,2]{0,2,1:T(2,128)} %copy.65) | data formatting | bytes 8388608 | tf_op jit(solution)/shard_map/reshape | solution.py:83
  116.2 5.5 %copy.66 = f32[512,2048]{1,0:T(8,128)} copy(f32[512,2048]{0,1:T(8,128)} %reshape.311) | data formatting | bytes 8388608 | tf_op jit(solution)/shard_map/reshape | solution.py:83
  121.7 4.9 multiply_reduce_fusion.1
  126.7 4.6 multiply_reduce_fusion
  133.7 5.2 convolution_convert_fusion.1
  140.3 4.2 fusion.38
  144.8 5.1 fusion.37
  151.2 13.3 %while.28 = (s32[]{:T(128)}, f32[4,1024]{1,0:T(4,128)S(1)}, f32[4,1024]{1,0:T(4,128)S(1)}, f32[4,1024,128]{1,2,0:T(8,128)}, bf16[4,1024,128]{2,1,0:T(8,128)(2,1)...) while((s32[]{:T(128)}, f32[4,1024]{1,0:T(4,128)S(1)}, ...), condition=%wide.region_5.6_spmd.clone, body=%wide.region_2.5_spmd.clone.sunk | while | flops 274200576 | bytes 7383157 | solution.py:117
  164.6 3.3 pad_maximum_fusion.2
  167.8 6.3 %copy.70 = f32[1024,1,520]{2,1,0:T(1,128)} copy(f32[1024,1,520]{0,2,1:T(8,128)} %pad_maximum_fusion.2) | data formatting | bytes 4259840 | tf_op jit(solution)/shard_map/concatenate | solution.py:36
  174.1 72.6 %all_to_all.45 = f32[1024,1,520]{2,1,0:T(1,128)S(1)} all-to-all(f32[1024,1,520]{2,1,0:T(1,128)} %copy.70), channel_id=1, replica_groups=mesh['ctx'=64,'lat'=4] {'ctx'}, dimensions={0} | all-to-all | bytes 4259840 | tf_op jit(solution)/shard_map/all_to_all | solution.py:39
  250.8 3.1 mul.170
  254.0 3.0 fusion.25
  258.3 4.3 all-to-all-start.3
  262.6 9.2 %all-to-all-done.3 = f32[4,16,2048]{2,1,0:T(8,128)S(1)} async-done(((f32[4,16,2048]{2,1,0:T(8,128)}), f32[4,16,2048]{2,1,0:T(8,128)S(1)}, u32[]{:S(2)}, u32[]{:S(2)}) %all-to-all-start.3) | async-done | bytes 524320 | tf_op jit(solution)/shard_map/all_to_all | solution.py:15
  280.6 71.2 %all-gather.6.cloned.1.call-done = bf16[1024,1024]{1,0:T(8,128)(2,1)} async-done(((bf16[16,1024]{1,0:T(8,128)(2,1)}), bf16[1024,1024]{1,0:T(8,128)(2,1)}) %all-gather.6.cloned.1.call-update) | async-done | bytes 2097168 | tf_op jit(solution)/shard_map/all_gather | solution.py:56
  355.0 6.8 %while.29 = (s32[]{:T(128)}, f32[4,16]{1,0:T(4,128)S(1)}, f32[4,16,128]{2,1,0:T(8,128)S(1)}, bf16[4,16,128]{2,1,0:T(8,128)(2,1)S(1)}, bf16[4,1024,128]{2,1,0:T(8...) while((s32[]{:T(128)}, f32[4,16]{1,0:T(4,128)S(1)}, ...), condition=%wide.region_14.15_spmd.clone, body=%wide.region_11.14_spmd.clone.sunk | while | flops 8552418 | bytes 736673 | solution.py:117
  364.0 10.1 %all_to_all.46 = bf16[4,16,2048]{2,1,0:T(8,128)(2,1)S(1)} all-to-all(bf16[4,16,2048]{2,1,0:T(8,128)(2,1)S(1)} %broadcast_in_dim.106), channel_id=1, replica_groups=mesh['ctx'=64,'lat'=4] {'lat'}, dimensions={0} | all-to-all | bytes 524288 | tf_op jit(solution)/shard_map/all_to_all | solution.py:15
  375.8 76.2 %all-gather.8.cloned.1.call-done = bf16[1024,2048]{1,0:T(8,128)(2,1)} async-done(((bf16[16,2048]{1,0:T(8,128)(2,1)}), bf16[1024,2048]{1,0:T(8,128)(2,1)}) %all-gather.8.cloned.1.call-update) | async-done | bytes 4194320 | tf_op jit(solution)/shard_map/all_gather | solution.py:204
  452.0 3.5 fusion.69
  458.1 2.9 reshape.318
  461.0 57.5 %all_to_all.47 = f32[64,4,2048]{2,1,0:T(4,128)} all-to-all(f32[64,4,2048]{2,1,0:T(4,128)} %reshape.318), channel_id=1, replica_groups=mesh['ctx'=64,'lat'=4] {'ctx'}, dimensions={0} | all-to-all | bytes 4194304 | tf_op jit(solution)/shard_map/all_to_all | solution.py:71
  518.5 2.5 reduce_sum.107
  (100 shorter events, 55.5 us)
Async XLA Ops:
  6.5 250.5 %copy-start = (bf16[512,2048]{1,0:T(8,128)(2,1)S(1)}, bf16[512,2048]{1,0:T(8,128)(2,1)}, u32[]{:S(2)}) copy-start(bf16[512,2048]{1,0:T(8,128)(2,1)} %param.19) | copy-start | bytes 6291460
  6.5 133.8 %all-gather.4.cloned.1.call-start = ((), (), s32[]{:S(2)}) async-start(), calls=%async_computation.6 | async-start | bytes 4259840 | tf_op jit(solution)/shard_map/all_gather | solution.py:149
  33.6 100.2 %all-to-all-start.1 = ((bf16[64,32,512]{2,1,0:T(8,128)(2,1)}), bf16[64,32,512]{2,1,0:T(8,128)(2,1)}, u32[]{:S(2)}, u32[]{:S(2)}) async-start(bf16[64,32,512]{2,1,0:T(8,128)(2,1)} %broadcast_in_dim.54), calls=%async_computation.1 | async-start | bytes 4194304 | tf_op jit(solution)/shard_map/all_to_all | solution.py:15
  116.2 5.5 %copy-start.2 = (bf16[256,2048]{1,0:T(8,128)(2,1)S(1)}, bf16[256,2048]{1,0:T(8,128)(2,1)}, u32[]{:S(2)}) copy-start(bf16[256,2048]{1,0:T(8,128)(2,1)} %param.16) | copy-start | bytes 3145732
  116.2 5.5 %copy-start.4 = (s32[512]{0:T(512)S(1)}, s32[512]{0:T(512)}, u32[]{:S(2)}) copy-start(s32[512]{0:T(512)} %param.14) | copy-start | bytes 6148
  246.8 1.5 copy-start.1
  258.3 13.5 %all-to-all-start.3 = ((f32[4,16,2048]{2,1,0:T(8,128)}), f32[4,16,2048]{2,1,0:T(8,128)S(1)}, u32[]{:S(2)}, u32[]{:S(2)}) async-start(f32[4,16,2048]{2,1,0:T(8,128)} %broadcast_in_dim.58), calls=%async_computation.3 | async-start | bytes 1048576 | tf_op jit(solution)/shard_map/all_to_all | solution.py:15
  262.6 89.2 %all-gather.6.cloned.1.call-start = ((), (), s32[]{:S(2)}) async-start(), calls=%async_computation.7 | async-start | bytes 2129920 | tf_op jit(solution)/shard_map/all_gather | solution.py:56
  278.3 173.7 %all-gather.8.cloned.1.call-start = ((), (), s32[]{:S(2)}) async-start(), calls=%async_computation.8 | async-start | bytes 4259840 | tf_op jit(solution)/shard_map/all_gather | solution.py:204
  361.9 90.2 %copy-start.3 = (bf16[128,2048]{1,0:T(8,128)(2,1)S(1)}, bf16[128,2048]{1,0:T(8,128)(2,1)}, u32[]{:S(2)}) copy-start(bf16[128,2048]{1,0:T(8,128)(2,1)} %param.23) | copy-start | bytes 1572868
Sparse Core Ops, SparseCore 0:
  10.2 92.9 all-gather.3
  278.4 73.3 all-gather.5
  375.9 76.0 all-gather.7
where the time goes:
time: 533 us; the launch traced here: 528 us
  blocking collectives  163 us (31%)
  waiting for transfers between devices  157 us (29%)
  local copies, waits for them, and re-layouts  81.8 us (15%)
  matrix products  52.1 us (10%)
  other arithmetic  48.5 us (9%)
  between operations  14.2 us (3%)
  starting transfers between devices  10.4 us (2%)
    all_gather x1, waiting for transfers between devices, per_device(): gathered = lax.all_gather(mlp_normed, 'ctx', axis=0, tiled=True)  76.2 us
    all_to_all x1, blocking collectives, side_by_side(): lax.all_to_all(both, axis, split_axis=split_dim, concat_axis=concat_dim,...  72.6 us
    all_gather x1, waiting for transfers between devices, side_by_side_2(): lax.all_gather(both, axis, axis=dim, tiled=True)  71.2 us
    all_to_all x1, blocking collectives, sent_and_summed(): lax.all_to_all(in_blocks(array, dim, count), axis, 0, 0, tiled=True)  57.5 us
    all_to_all x2, blocking collectives, sent_to_all(): lax.all_to_all(jnp.broadcast_to(array[None], (count, *array.shape)), axis...  33.2 us
    reshape x4, local copies, waits for them, and re-layouts, sinusoid(): jnp.stack([jnp.sin(angles), jnp.cos(angles)], axis=-1)  32.2 us
    sin x2, other arithmetic, sinusoid(): jnp.sin(angles)  22.2 us
    another operation x2, local copies, waits for them, and re-layouts, sinusoid(): jnp.stack([jnp.sin(angles), jnp.cos(angles)], axis=-1)  20.8 us
  transfers between devices with their start and end apart: 5, of which 3 were waited for; matrix products, arithmetic and copies ran while one was open for 20% of the time, Pallas kernels for 0%

commit v1 on v0

--- a/solution.py
+++ b/solution.py
@@ -201,7 +201,9 @@
         "lat",
     ).astype(jnp.float32)
     mlp_normed = rms_normalize(second_stream).astype(jnp.bfloat16)
-    gathered = lax.all_gather(mlp_normed, "ctx", axis=0, tiled=True)
+    gathered = jnp.concatenate(
+        lax.all_to_all(jnp.stack([mlp_normed] * lax.axis_size("ctx")), "ctx", 0, 0), axis=0
+    )
     group_input = lax.dynamic_slice_in_dim(gathered, group_index * group_rows, group_rows, 0)
     pre_hidden = jnp.dot(group_input, mlp_in, preferred_element_type=jnp.float32)
     hidden = jax.nn.gelu(pre_hidden, approximate=True).astype(jnp.bfloat16)

time: 533 us -> 562 us (1.054)
  waiting for transfers between devices: 157 us -> 177 us
  starting transfers between devices: 10.4 us -> 18.5 us
    all_to_all x0 -> x1, waiting for transfers between devices: none -> 95.9 us  [per_device(): lax.all_to_all(jnp.stack([mlp_normed] * lax.axis_size('ctx')), 'ctx', 0, 0)]
    all_gather x1 -> x0, waiting for transfers between devices: 76.2 us -> none  [per_device(): gathered = lax.all_gather(mlp_normed, 'ctx', axis=0, tiled=True)]
    all_to_all x0 -> x1, starting transfers between devices: none -> 8.13 us  [per_device(): lax.all_to_all(jnp.stack([mlp_normed] * lax.axis_size('ctx')), 'ctx', 0, 0)]
  transfers between devices with their start and end apart: 5 -> 5, of which waited for: 3 -> 3; matrix products, arithmetic and copies ran while one was open for 20% -> 19% of each run, Pallas kernels for 0% -> 0%
where the time goes in v1:
time: 562 us; the launch traced here: 557 us
  waiting for transfers between devices  177 us (31%)
  blocking collectives  163 us (29%)
  local copies, waits for them, and re-layouts  84.3 us (15%)
  matrix products  51.9 us (9%)
  other arithmetic  47.8 us (9%)
  starting transfers between devices  18.5 us (3%)
  between operations  14.6 us (3%)
    all_to_all x1, waiting for transfers between devices, per_device(): lax.all_to_all(jnp.stack([mlp_normed] * lax.axis_size('ctx')), 'ctx', 0, 0)  95.9 us
    all_to_all x1, blocking collectives, side_by_side(): lax.all_to_all(both, axis, split_axis=split_dim, concat_axis=concat_dim,...  72.6 us
    all_gather x1, waiting for transfers between devices, side_by_side_2(): lax.all_gather(both, axis, axis=dim, tiled=True)  71.5 us
    all_to_all x1, blocking collectives, sent_and_summed(): lax.all_to_all(in_blocks(array, dim, count), axis, 0, 0, tiled=True)  57 us
    all_to_all x2, blocking collectives, sent_to_all(): lax.all_to_all(jnp.broadcast_to(array[None], (count, *array.shape)), axis...  33.2 us
    reshape x4, local copies, waits for them, and re-layouts, sinusoid(): jnp.stack([jnp.sin(angles), jnp.cos(angles)], axis=-1)  32.2 us
    sin x2, other arithmetic, sinusoid(): jnp.sin(angles)  22.2 us
    another operation x2, local copies, waits for them, and re-layouts, sinusoid(): jnp.stack([jnp.sin(angles), jnp.cos(angles)], axis=-1)  20.8 us
  transfers between devices with their start and end apart: 5, of which 3 were waited for; matrix products, arithmetic and copies ran while one was open for 19% of the time, Pallas kernels for 0%

profile of v1, /device:TPU:1, one launch (start us, length us, event | category | flops | bytes accessed | tf_op | source)
XLA Modules:
  0.0 557.0 jit_solution(4517891871602698431)
XLA Ops:
  8.0 23.1 %all_to_all.49 = s32[64,1,512]{2,1,0:T(1,128)S(1)} all-to-all(s32[64,1,512]{2,1,0:T(1,128)S(1)} %broadcast_in_dim.52), channel_id=1, replica_groups=mesh['ctx'=64,'lat'=4] {'ctx'}, dimensions={0} | all-to-all | bytes 262144 | tf_op jit(solution)/shard_map/all_to_all | solution.py:15
  33.6 5.8 %all-to-all-start.1 = ((bf16[64,32,512]{2,1,0:T(8,128)(2,1)}), bf16[64,32,512]{2,1,0:T(8,128)(2,1)}, u32[]{:S(2)}, u32[]{:S(2)}) async-start(bf16[64,32,512]{2,1,0:T(8,128)(2,1)} %broadcast_in_dim.54), calls=%async_computation.1 | async-start | bytes 4194304 | tf_op jit(solution)/shard_map/all_to_all | solution.py:15
  40.1 14.9 %multiply_sine_fusion = (f32[1024,1024,1]{1,0,2:T(8,128)S(1)}, f32[1024,1024,1]{1,0,2:T(8,128)S(1)}) fusion(f32[1024]{0:T(1024)S(1)} %multiply_exponential_fusion, f32[1024]{0:T(1024)S(1)} %get-tuple-element.184), kind=kLoop, calls=%fused_computation.36 | loop fusion | flops 1048576 | bytes 8396800 | tf_op jit(solution)/shard_map/sin | solution.py:83
  55.0 4.1 pad_maximum_fusion
  59.0 13.6 %copy.62 = f32[1024,1024,2]{0,2,1:T(2,128)} copy(f32[1024,1024,2]{1,0,2:T(8,128)} %pad_maximum_fusion) | data formatting | bytes 16777216 | tf_op jit(solution)/shard_map/stack | solution.py:83
  72.6 10.9 %reshape.313 = f32[1024,2048]{0,1:T(8,128)} reshape(f32[1024,1024,2]{0,2,1:T(2,128)} %copy.62) | data formatting | bytes 16777216 | tf_op jit(solution)/shard_map/reshape | solution.py:83
  83.5 9.7 %copy.63 = f32[1024,2048]{1,0:T(8,128)} copy(f32[1024,2048]{0,1:T(8,128)} %reshape.313) | data formatting | bytes 16777216 | tf_op jit(solution)/shard_map/reshape | solution.py:83
  93.2 7.3 %multiply_sine_fusion.1 = (f32[512,1024,1]{1,0,2:T(8,128)S(1)}, f32[512,1024,1]{1,0,2:T(8,128)S(1)}) fusion(f32[1024]{0:T(1024)S(1)} %multiply_exponential_fusion, f32[512]{0:T(512)S(1)} %get-tuple-element.186), kind=kLoop, calls=%fused_computation.43 | loop fusion | flops 524288 | bytes 4200448 | tf_op jit(solution)/shard_map/sin | solution.py:83
  102.8 7.3 %copy.65 = f32[512,1024,2]{0,2,1:T(2,128)} copy(f32[512,1024,2]{1,0,2:T(8,128)} %pad_maximum_fusion.1) | data formatting | bytes 8388608 | tf_op jit(solution)/shard_map/stack | solution.py:83
  110.1 6.1 %reshape.316 = f32[512,2048]{0,1:T(8,128)} reshape(f32[512,1024,2]{0,2,1:T(2,128)} %copy.65) | data formatting | bytes 8388608 | tf_op jit(solution)/shard_map/reshape | solution.py:83
  116.2 5.5 copy.66
  121.7 4.9 multiply_reduce_fusion.1
  126.7 4.6 multiply_reduce_fusion
  133.7 5.2 convolution_convert_fusion.1
  140.3 4.2 fusion.38
  144.8 5.1 fusion.37
  151.2 13.3 %while.28 = (s32[]{:T(128)}, f32[4,1024]{1,0:T(4,128)S(1)}, f32[4,1024]{1,0:T(4,128)S(1)}, f32[4,1024,128]{1,2,0:T(8,128)}, bf16[4,1024,128]{2,1,0:T(8,128)(2,1)...) while((s32[]{:T(128)}, f32[4,1024]{1,0:T(4,128)S(1)}, ...), condition=%wide.region_5.6_spmd.clone, body=%wide.region_2.5_spmd.clone.sunk | while | flops 274200576 | bytes 7383157 | solution.py:117
  164.6 3.3 pad_maximum_fusion.2
  167.8 6.3 %copy.70 = f32[1024,1,520]{2,1,0:T(1,128)} copy(f32[1024,1,520]{0,2,1:T(8,128)} %pad_maximum_fusion.2) | data formatting | bytes 4259840 | tf_op jit(solution)/shard_map/concatenate | solution.py:36
  174.1 72.6 %all_to_all.50 = f32[1024,1,520]{2,1,0:T(1,128)S(1)} all-to-all(f32[1024,1,520]{2,1,0:T(1,128)} %copy.70), channel_id=1, replica_groups=mesh['ctx'=64,'lat'=4] {'ctx'}, dimensions={0} | all-to-all | bytes 4259840 | tf_op jit(solution)/shard_map/all_to_all | solution.py:39
  250.8 3.1 mul.170
  254.0 3.0 fusion.25
  258.3 4.3 all-to-all-start.3
  262.8 8.9 %all-to-all-done.3 = f32[4,16,2048]{2,1,0:T(8,128)S(1)} async-done(((f32[4,16,2048]{2,1,0:T(8,128)}), f32[4,16,2048]{2,1,0:T(8,128)S(1)}, u32[]{:S(2)}, u32[]{:S(2)}) %all-to-all-start.3) | async-done | bytes 524320 | tf_op jit(solution)/shard_map/all_to_all | solution.py:15
  280.3 71.5 %all-gather.5.cloned.1.call-done = bf16[1024,1024]{1,0:T(8,128)(2,1)} async-done(((bf16[16,1024]{1,0:T(8,128)(2,1)}), bf16[1024,1024]{1,0:T(8,128)(2,1)}) %all-gather.5.cloned.1.call-update) | async-done | bytes 2097168 | tf_op jit(solution)/shard_map/all_gather | solution.py:56
  355.0 6.8 %while.29 = (s32[]{:T(128)}, f32[4,16]{1,0:T(4,128)S(1)}, f32[4,16,128]{2,1,0:T(8,128)S(1)}, bf16[4,16,128]{2,1,0:T(8,128)(2,1)S(1)}, bf16[4,1024,128]{2,1,0:T(8...) while((s32[]{:T(128)}, f32[4,16]{1,0:T(4,128)S(1)}, ...), condition=%wide.region_14.15_spmd.clone, body=%wide.region_11.14_spmd.clone.sunk | while | flops 8552418 | bytes 736673 | solution.py:117
  363.9 10.1 %all_to_all.51 = bf16[4,16,2048]{2,1,0:T(8,128)(2,1)S(1)} all-to-all(bf16[4,16,2048]{2,1,0:T(8,128)(2,1)S(1)} %broadcast_in_dim.106), channel_id=1, replica_groups=mesh['ctx'=64,'lat'=4] {'lat'}, dimensions={0} | all-to-all | bytes 524288 | tf_op jit(solution)/shard_map/all_to_all | solution.py:15
  377.6 8.1 %all-to-all-start.5 = ((bf16[64,16,2048]{2,1,0:T(8,128)(2,1)}), bf16[64,16,2048]{2,1,0:T(8,128)(2,1)}, u32[]{:S(2)}, u32[]{:S(2)}) async-start(bf16[64,16,2048]{2,1,0:T(8,128)(2,1)} %stack.8), calls=%async_computation.5 | async-start | bytes 8388608 | tf_op jit(solution)/shard_map/all_to_all | solution.py:205
  385.7 95.9 %all-to-all-done.5 = bf16[64,16,2048]{2,1,0:T(8,128)(2,1)} async-done(((bf16[64,16,2048]{2,1,0:T(8,128)(2,1)}), bf16[64,16,2048]{2,1,0:T(8,128)(2,1)}, u32[]{:S(2)}, u32[]{:S(2)}) %all-to-all-start.5) | async-done | bytes 4194336 | tf_op jit(solution)/shard_map/all_to_all | solution.py:205
  481.6 3.3 fusion.69
  487.6 2.9 reshape.324
  490.5 57.0 %all_to_all.52 = f32[64,4,2048]{2,1,0:T(4,128)} all-to-all(f32[64,4,2048]{2,1,0:T(4,128)} %reshape.324), channel_id=1, replica_groups=mesh['ctx'=64,'lat'=4] {'ctx'}, dimensions={0} | all-to-all | bytes 4194304 | tf_op jit(solution)/shard_map/all_to_all | solution.py:71
  (102 shorter events, 59.7 us)
Async XLA Ops:
  6.5 250.5 %copy-start = (bf16[512,2048]{1,0:T(8,128)(2,1)S(1)}, bf16[512,2048]{1,0:T(8,128)(2,1)}, u32[]{:S(2)}) copy-start(bf16[512,2048]{1,0:T(8,128)(2,1)} %param.19) | copy-start | bytes 6291460
  6.5 133.8 %all-gather.3.cloned.1.call-start = ((), (), s32[]{:S(2)}) async-start(), calls=%async_computation.7 | async-start | bytes 4259840 | tf_op jit(solution)/shard_map/all_gather | solution.py:149
  33.6 100.2 %all-to-all-start.1 = ((bf16[64,32,512]{2,1,0:T(8,128)(2,1)}), bf16[64,32,512]{2,1,0:T(8,128)(2,1)}, u32[]{:S(2)}, u32[]{:S(2)}) async-start(bf16[64,32,512]{2,1,0:T(8,128)(2,1)} %broadcast_in_dim.54), calls=%async_computation.1 | async-start | bytes 4194304 | tf_op jit(solution)/shard_map/all_to_all | solution.py:15
  116.2 5.5 copy-start.2
  116.2 5.5 copy-start.5
  246.8 1.5 copy-start.1
  258.3 13.5 %all-to-all-start.3 = ((f32[4,16,2048]{2,1,0:T(8,128)}), f32[4,16,2048]{2,1,0:T(8,128)S(1)}, u32[]{:S(2)}, u32[]{:S(2)}) async-start(f32[4,16,2048]{2,1,0:T(8,128)} %broadcast_in_dim.58), calls=%async_computation.3 | async-start | bytes 1048576 | tf_op jit(solution)/shard_map/all_to_all | solution.py:15
  262.6 89.2 %all-gather.5.cloned.1.call-start = ((), (), s32[]{:S(2)}) async-start(), calls=%async_computation.8 | async-start | bytes 2129920 | tf_op jit(solution)/shard_map/all_gather | solution.py:56
  377.6 104.0 %copy-start.3 = (bf16[128,2048]{1,0:T(8,128)(2,1)S(1)}, bf16[128,2048]{1,0:T(8,128)(2,1)}, u32[]{:S(2)}) copy-start(bf16[128,2048]{1,0:T(8,128)(2,1)} %param.23) | copy-start | bytes 1572868
  377.6 104.0 %copy-start.4 = (bf16[2048,128]{1,0:T(8,128)(2,1)S(1)}, bf16[2048,128]{1,0:T(8,128)(2,1)}, u32[]{:S(2)}) copy-start(bf16[2048,128]{1,0:T(8,128)(2,1)} %param.22) | copy-start | bytes 1572868
  377.6 104.0 %all-to-all-start.5 = ((bf16[64,16,2048]{2,1,0:T(8,128)(2,1)}), bf16[64,16,2048]{2,1,0:T(8,128)(2,1)}, u32[]{:S(2)}, u32[]{:S(2)}) async-start(bf16[64,16,2048]{2,1,0:T(8,128)(2,1)} %stack.8), calls=%async_computation.5 | async-start | bytes 8388608 | tf_op jit(solution)/shard_map/all_to_all | solution.py:205
Sparse Core Ops, SparseCore 0:
  10.2 92.9 all-gather.2
  278.4 73.3 all-gather.4
